TPU v7x, 32 devices: a whole 2x2x4 slice. The times are simulated.
32 devices in a mesh: out: 4 (over z), in: 8 (over y, x, core).
Axes of the slice: x: 2, y: 2, z: 4, core: 2. Of those that a mesh axis runs over, the one named last changes fastest.
Arguments:
- tensor: bfloat16 [1024, 1024, 1024], P('out', 'in'), may hold values from -0.0078125 to 0.0078125
- linear: bfloat16 [1024, 1024], P('out', 'in'), may hold values from -0.1875 to 0.1875
- adjoint_end: float32 [128, 1024], P(None, 'in'), may hold values from -6 to 6
- states: bfloat16 [2, 128, 1024], replicated, may hold values from -6 to 6
Outputs:
- adjoint_start: float32 [128, 1024], P(None, 'in')
All inputs are finite; a program needn't handle non-finite values.
Results may differ from a plain program's by a relative error of at most 0.0045.
Values may be sent and summed in bfloat16 or wider, within the bound.
A program may use at most 128 MiB of HBM per device.

v0:
```python
import jax
import jax.numpy as jnp
from jax import lax
from jax.sharding import PartitionSpec as P

step_size = 0.5


def pieces(tensor, linear, state, full_low):
    rows_block = tensor.shape[0]
    cols_block = tensor.shape[1]
    modes = tensor.shape[2]
    batch = full_low.shape[0]
    lam_rows = lax.dynamic_slice_in_dim(full_low, lax.axis_index("out") * rows_block, rows_block, 1)
    state_cols = lax.dynamic_slice_in_dim(state, lax.axis_index("in") * cols_block, cols_block, 1)
    flat = tensor.reshape(rows_block * cols_block, modes)
    projected = lax.dot_general(
        state, flat, (((1,), (1,)), ((), ())), preferred_element_type=jnp.float32
    )
    projected = projected.reshape(batch, rows_block, cols_block)
    lam_float = lam_rows.astype(jnp.float32)
    first = jnp.einsum("bi,bij->bj", lam_float, projected)
    lin = jnp.dot(lam_rows, linear, preferred_element_type=jnp.float32)
    pair = (lam_float[:, :, None] * state_cols.astype(jnp.float32)[:, None, :]).astype(jnp.bfloat16)
    second = jnp.dot(
        pair.reshape(batch, rows_block * cols_block), flat, preferred_element_type=jnp.float32
    )
    return (lin + first, second)


def per_device(tensor, linear, adjoint_end, states):
    steps_total = states.shape[0]
    lam_own = adjoint_end
    for number in range(steps_total - 1, -1, -1):
        full_low = lax.all_gather(lam_own.astype(jnp.bfloat16), "in", axis=1, tiled=True)
        local, second = pieces(tensor, linear, states[number], full_low)
        second_own = lax.psum_scatter(second, "in", scatter_dimension=1, tiled=True)
        total = lax.psum(local + second_own, "out")
        lam_own = lam_own + step_size * total
    return lam_own


def solution(mesh):
    placed = (P("out", "in", None), P("out", "in"), P(None, "in"), P())
    return jax.shard_map(
        per_device, mesh=mesh, in_specs=placed, out_specs=P(None, "in"), check_vma=False
    )
```

profile of v0, /device:TPU:0, one launch (start us, length us, event | category | flops | bytes accessed | tf_op | source)
XLA Modules:
  0.0 240.2 jit_solution(15513194253521051072)
XLA Ops:
  6.5 0.0 copy-start
  6.5 0.0 reduce-scatter.3.cloned.1.call-start
  6.5 1.1 fusion.27
  7.6 0.8 convert_element_type.38
  8.5 10.8 %all_gather.6 = bf16[128,1024]{1,0:T(8,128)(2,1)S(1)} all-gather(bf16[128,128]{1,0:T(8,128)(2,1)S(1)} %convert_element_type.38), channel_id=1, replica_groups=mesh['out'=4,'in'=8] {'in'}, dimensions={1}, use_global_device_ids=true | all-gather | bytes 294912 | tf_op jit(solution)/shard_map/all_gather | solution.py:35
  19.3 0.1 copy.5
  19.4 0.0 copy-start.1
  19.5 22.1 %fusion.11 = f32[128,1024]{1,0:T(8,128)} fusion(bf16[256,128,1024]{2,1,0:T(8,128)(2,1)} %param.4, f32[128,128]{1,0:T(8,128)S(1)} %bitcast_convert_fusion.1, f32[128,256]{0,1:T(8,128)S(1)} %copy.5), kind=kOutput, calls=%fused_computation.13 | convolution fusion | flops 8598323200 | bytes 67829760 | tf_op jit(solution)/shard_map/dot_general | solution.py:25
  41.5 0.0 reduce-scatter.3.cloned.1.call-update
  41.6 0.0 copy-start.2
  41.6 0.0 all-reduce.3.cloned.1.call-start
  41.6 0.0 copy-done.1
  41.6 32.5 %fusion.16 = bf16[128,256,128]{2,0,1:T(8,128)(2,1)} fusion(bf16[256,128,1024]{2,1,0:T(8,128)(2,1)} %param.4, bf16[2,128,1024]{2,1,0:T(8,128)(2,1)S(1)} %copy-done.1), kind=kOutput, calls=%fused_computation.20 | convolution fusion | flops 8589934592 | bytes 75759616 | tf_op jit(solution)/shard_map/dot_general | solution.py:17
  74.1 11.2 %fusion.2 = f32[128,1,128]{2,1,0:T(1,128)S(1)} fusion(bf16[128,256,128]{2,0,1:T(8,128)(2,1)} %fusion.16, bf16[128,256,1]{1,0,2:T(8,128)(2,1)S(1)} %get-tuple-element.9), kind=kOutput, calls=%fused_computation.2 | convolution fusion | flops 8388608 | bytes 8519680 | tf_op jit(solution)/shard_map/bi,bij->bj/dot_general | solution.py:22
  85.3 0.0 reduce-scatter.3.cloned.1.call-done
  85.3 0.0 copy-done
  85.3 1.6 fusion.13
  86.9 0.0 all-reduce.3.cloned.1.call-update
  86.9 0.0 reduce-scatter.5.cloned.1.call-start
  87.0 34.4 %all-reduce.3.cloned.1.call-done = f32[128,128]{1,0:T(8,128)} async-done(((f32[128,128]{1,0:T(8,128)}), f32[128,128]{1,0:T(8,128)}) %all-reduce.3.cloned.1.call-update) | async-done | bytes 65552 | tf_op jit(solution)/shard_map/psum | solution.py:38
  121.4 0.0 copy-done.2
  121.4 0.8 fusion.22
  122.3 9.3 %all_gather.7 = bf16[128,1024]{1,0:T(8,128)(2,1)S(1)} all-gather(bf16[128,128]{1,0:T(8,128)(2,1)S(1)} %fusion.22), channel_id=1, replica_groups=mesh['out'=4,'in'=8] {'in'}, dimensions={1}, use_global_device_ids=true | all-gather | bytes 294912 | tf_op jit(solution)/shard_map/all_gather | solution.py:35
  131.6 0.1 copy.6
  131.7 22.0 %fusion.10 = f32[128,1024]{1,0:T(8,128)} fusion(bf16[256,128,1024]{2,1,0:T(8,128)(2,1)} %param.4, f32[128,128]{1,0:T(8,128)S(1)} %bitcast_convert_fusion, f32[128,256]{0,1:T(8,128)S(1)} %copy.6), kind=kOutput, calls=%fused_computation.12 | convolution fusion | flops 8598323200 | bytes 67829760 | tf_op jit(solution)/shard_map/dot_general | solution.py:25
  153.7 0.0 reduce-scatter.5.cloned.1.call-update
  153.8 0.0 copy-start.3
  153.8 0.2 all-reduce.5.cloned.1.call-start
  154.0 32.4 %fusion.14 = bf16[128,256,128]{2,0,1:T(8,128)(2,1)} fusion(bf16[256,128,1024]{2,1,0:T(8,128)(2,1)} %param.4, bf16[2,128,1024]{2,1,0:T(8,128)(2,1)S(1)} %copy-done.1), kind=kOutput, calls=%fused_computation.18 | convolution fusion | flops 8589934592 | bytes 75759616 | tf_op jit(solution)/shard_map/dot_general | solution.py:17
  186.4 11.2 %fusion = f32[128,1,128]{2,1,0:T(1,128)S(1)} fusion(bf16[128,256,128]{2,0,1:T(8,128)(2,1)} %fusion.14, bf16[128,256,1]{1,0,2:T(8,128)(2,1)S(1)} %get-tuple-element.7), kind=kOutput, calls=%fused_computation | convolution fusion | flops 8388608 | bytes 8519680 | tf_op jit(solution)/shard_map/bi,bij->bj/dot_general | solution.py:22
  197.6 0.0 reduce-scatter.5.cloned.1.call-done
  197.6 1.6 fusion.12
  199.2 0.0 all-reduce.5.cloned.1.call-update
  199.2 33.0 %all-reduce.5.cloned.1.call-done = f32[128,128]{1,0:T(8,128)} async-done(((f32[128,128]{1,0:T(8,128)}), f32[128,128]{1,0:T(8,128)}) %all-reduce.5.cloned.1.call-update) | async-done | bytes 65552 | tf_op jit(solution)/shard_map/psum | solution.py:38
  232.2 0.0 copy-done.3
  232.2 1.5 multiply_add_fusion
  (4 shorter events, 0.1 us)
Async XLA Ops:
  6.5 78.8 %copy-start = (bf16[256,128]{1,0:T(8,128)(2,1)S(1)}, bf16[256,128]{1,0:T(8,128)(2,1)}, u32[]{:S(2)}) copy-start(bf16[256,128]{1,0:T(8,128)(2,1)} %param.5) | copy-start | bytes 196612
  6.5 78.7 %reduce-scatter.3.cloned.1.call-start = ((), (), s32[]{:S(2)}) async-start(), calls=%async_computation.2 | async-start | bytes 589824 | tf_op jit(solution)/shard_map/reduce_scatter | solution.py:37
  19.4 22.2 %copy-start.1 = (bf16[2,128,1024]{2,1,0:T(8,128)(2,1)S(1)}, bf16[2,128,1024]{2,1,0:T(8,128)(2,1)}, u32[]{:S(2)}) copy-start(bf16[2,128,1024]{2,1,0:T(8,128)(2,1)} %param.7) | copy-start | bytes 1572868
  41.6 79.9 %copy-start.2 = (f32[128,128]{1,0:T(8,128)S(1)}, f32[128,128]{1,0:T(8,128)}, u32[]{:S(2)}) copy-start(f32[128,128]{1,0:T(8,128)} %param.6) | copy-start | bytes 196612
  41.6 79.8 %all-reduce.3.cloned.1.call-start = ((), (), s32[]{:S(2)}) async-start(), calls=%async_computation.3 | async-start | bytes 131072 | tf_op jit(solution)/shard_map/psum | solution.py:38
  86.9 110.6 %reduce-scatter.5.cloned.1.call-start = ((), (), s32[]{:S(2)}) async-start(), calls=%async_computation.4 | async-start | bytes 589824 | tf_op jit(solution)/shard_map/reduce_scatter | solution.py:37
  153.8 78.5 %copy-start.3 = (f32[128,128]{1,0:T(8,128)S(1)}, f32[128,128]{1,0:T(8,128)}, u32[]{:S(2)}) copy-start(f32[128,128]{1,0:T(8,128)} %all-reduce.3.cloned.1.call-done) | copy-start | bytes 196612
  153.8 78.5 %all-reduce.5.cloned.1.call-start = ((), (), s32[]{:S(2)}) async-start(), calls=%async_computation.5 | async-start | bytes 131072 | tf_op jit(solution)/shard_map/psum | solution.py:38
Sparse Core Ops, SparseCore 0:
  41.7 34.4 reduce-scatter.2
  87.1 34.3 all-reduce.2
  153.9 32.9 reduce-scatter.4
  199.4 32.8 all-reduce.4
where the time goes:
time: 241 us; the launch traced here: 240 us
  matrix products  135 us (56%)
  waiting for transfers between devices  67.5 us (28%)
  blocking collectives  20.2 us (8%)
  between operations  13.2 us (5%)
  other arithmetic  3.25 us (1%)
    psum x2, waiting for transfers between devices, per_device(): total = lax.psum(local + second_own, 'out')  67.4 us
    dot_general x2, matrix products, pieces(): lax.dot_general(state, flat, (((1,), (1,)), ((), ())), preferred_element_...  64.9 us
    dot_general x2, matrix products, pieces(): jnp.dot(pair.reshape(batch, rows_block * cols_block), flat, preferred_ele...  44.1 us
    dot_general x2, matrix products, pieces(): first = jnp.einsum('bi,bij->bj', lam_float, projected)  22.4 us
    all_gather x2, blocking collectives, per_device(): lax.all_gather(lam_own.astype(jnp.bfloat16), 'in', axis=1, tiled=True)  20.2 us
  transfers between devices with their start and end apart: 4, of which 2 were waited for; matrix products, arithmetic and copies ran while one was open for 36% of the time, Pallas kernels for 0%

commit v1 on v0

--- a/solution.py
+++ b/solution.py
@@ -1,9 +1,16 @@
+import functools
+
 import jax
 import jax.numpy as jnp
 from jax import lax
+from jax.experimental import pallas as pl
+from jax.experimental.pallas import tpu as pltpu
 from jax.sharding import PartitionSpec as P
 
 step_size = 0.5
+MESH = pl.DeviceIdType.MESH
+tile_modes = 8
+slots = 18
 
 
 def pieces(tensor, linear, state, full_low):
@@ -28,7 +35,7 @@
     return (lin + first, second)
 
 
-def per_device(tensor, linear, adjoint_end, states):
+def plain(tensor, linear, adjoint_end, states):
     steps_total = states.shape[0]
     lam_own = adjoint_end
     for number in range(steps_total - 1, -1, -1):
@@ -40,8 +47,256 @@
     return lam_own
 
 
+def kernel(n_out, n_in, rows, cols,
+           flat_ref, linear_ref, adjoint_ref, states_ref, out_ref,
+           tbuf, kept, st, lowsrc, lowbuf, lowf, low_t, acc, first_t,
+           send1, recv1, part2, recv2, lamq, finrecv,
+           tsem, s1, r1, s2, r2, ls, lr, fs, fr):
+    batch = adjoint_ref.shape[0]
+    quarter = batch // n_out
+    ratio = rows // cols
+    tiles = rows // tile_modes
+    tile_rows = tile_modes * cols
+    held = tbuf.shape[0]
+    base = tiles - held
+    o = lax.axis_index("out")
+    c = lax.axis_index("in")
+    plane = c // ratio
+    part = lax.rem(c, ratio)
+
+    def load(number):
+        tile = lax.rem(number, tiles)
+        slot = lax.rem(number, held)
+        return pltpu.make_async_copy(
+            flat_ref.at[pl.ds(pl.multiple_of(tile * tile_rows, tile_rows), tile_rows)],
+            tbuf.at[slot], tsem.at[slot])
+
+    @pl.loop(0, held)
+    def _(number):
+        load(number).start()
+
+    barrier = pltpu.get_barrier_semaphore()
+    for d in range(1, n_in):
+        pl.semaphore_signal(barrier, inc=1, device_id=(o, lax.rem(c + d, n_in)), device_id_type=MESH)
+    for d in range(1, n_out):
+        pl.semaphore_signal(barrier, inc=1, device_id=(lax.rem(o + d, n_out), c), device_id_type=MESH)
+    for q in range(n_out):
+        for e in range(ratio):
+            source = o * ratio + e
+
+            @pl.when(jnp.logical_or(o != q, c != source))
+            def _():
+                pl.semaphore_signal(barrier, inc=1, device_id=(q, source), device_id_type=MESH)
+
+    @pl.when(plane == o)
+    def _():
+        pl.semaphore_wait(barrier, 2 * n_in + n_out - 3)
+
+    @pl.when(plane != o)
+    def _():
+        pl.semaphore_wait(barrier, 2 * n_in + n_out - 2)
+
+    def low_copy(step, x):
+        return pltpu.make_async_remote_copy(
+            src_ref=lowsrc.at[step], dst_ref=lowbuf.at[step, part, o],
+            send_sem=ls.at[step, x], recv_sem=lr.at[step, part, o],
+            device_id=(plane, x), device_id_type=MESH)
+
+    def low_start(step):
+        lowsrc[step] = lamq[...].astype(jnp.bfloat16)
+        for x in range(n_in):
+            @pl.when(jnp.logical_or(plane != o, c != x))
+            def _():
+                low_copy(step, x).start()
+
+        @pl.when(plane == o)
+        def _():
+            lowbuf[step, part, o] = lowsrc[step]
+
+    def low_wait(step):
+        for e in range(ratio):
+            for q in range(n_out):
+                @pl.when(jnp.logical_or(o != q, c != o * ratio + e))
+                def _():
+                    pltpu.make_async_remote_copy(
+                        src_ref=lowsrc.at[step], dst_ref=lowbuf.at[step, e, q],
+                        send_sem=ls.at[step, 0], recv_sem=lr.at[step, e, q],
+                        device_id=(plane, c), device_id_type=MESH).wait_recv()
+        for e in range(ratio):
+            block = lowbuf[step, e].reshape(batch, cols).astype(jnp.float32)
+            lowf[e] = block
+            low_t[e * cols:(e + 1) * cols] = block.T
+        for x in range(n_in):
+            @pl.when(jnp.logical_or(plane != o, c != x))
+            def _():
+                low_copy(step, x).wait_send()
+
+    def add_second(step, tile, slot):
+        per = cols // tile_modes
+        offset = lax.rem(tile, per) * tile_modes
+        turned = pltpu.roll(lowf[tile // per], lax.rem(cols - offset, cols), 1)
+        own = states_ref[step, :, pl.ds(pl.multiple_of(c * cols, cols), cols)].astype(jnp.float32)
+        pair = jnp.concatenate(
+            [(turned[:, q:q + 1] * own).astype(jnp.bfloat16) for q in range(tile_modes)], axis=1)
+        acc[...] += jnp.dot(pair, tbuf[slot], preferred_element_type=jnp.float32)
+
+    def add_first(tile, projected):
+        low = low_t[pl.ds(pl.multiple_of(tile * tile_modes, tile_modes), tile_modes)]
+        total = first_t[...]
+        for q in range(tile_modes):
+            total += low[q:q + 1] * projected[q * cols:(q + 1) * cols]
+        first_t[...] = total
+
+    def exchange(step):
+        for x in range(n_in):
+            send1[x] = acc[:, x * cols:(x + 1) * cols].astype(jnp.bfloat16)
+        copies = []
+        for d in range(1, n_in):
+            target = lax.rem(c + d, n_in)
+            copy = pltpu.make_async_remote_copy(
+                src_ref=send1.at[target], dst_ref=recv1.at[step, d],
+                send_sem=s1.at[step, d], recv_sem=r1.at[step, d],
+                device_id=(o, target), device_id_type=MESH)
+            copy.start()
+            copies.append(copy)
+        total = first_t[...].T + acc[:, pl.ds(pl.multiple_of(c * cols, cols), cols)]
+        for e in range(ratio):
+            total += jnp.dot(lowbuf[step, e].reshape(batch, cols), linear_ref[e * cols:(e + 1) * cols],
+                             preferred_element_type=jnp.float32)
+        for d in range(1, n_in):
+            copies[d - 1].wait_recv()
+            total += recv1[step, d].astype(jnp.float32)
+        part2[...] = total.reshape(n_out, quarter, cols)
+        for d in range(1, n_out):
+            target = lax.rem(o + d, n_out)
+            copy = pltpu.make_async_remote_copy(
+                src_ref=part2.at[target], dst_ref=recv2.at[step, d],
+                send_sem=s2.at[step, d], recv_sem=r2.at[step, d],
+                device_id=(target, c), device_id_type=MESH)
+            copy.start()
+            copies.append(copy)
+        mine = part2[o]
+        for d in range(1, n_out):
+            copies[n_in - 2 + d].wait_recv()
+            mine += recv2[step, d]
+        lamq[...] += step_size * mine
+        return copies
+
+    lamq[...] = adjoint_ref[pl.ds(pl.multiple_of(o * quarter, quarter), quarter)]
+    low_start(1)
+    st[:, :batch] = states_ref[1].T
+    st[:, batch:] = states_ref[0].T
+    acc[...] = jnp.zeros_like(acc)
+    first_t[...] = jnp.zeros_like(first_t)
+    low_wait(1)
+
+    @pl.loop(0, tiles)
+    def _(tile):
+        slot = lax.rem(tile, held)
+        load(tile).wait()
+        both = jnp.dot(tbuf[slot], st[...], preferred_element_type=jnp.float32)
+        kept[tile] = both[:, batch:]
+        add_first(tile, both[:, :batch])
+        add_second(1, tile, slot)
+
+        @pl.when(tile < base)
+        def _():
+            load(tile + held).start()
+
+    copies = exchange(1)
+    low_start(0)
+    acc[...] = jnp.zeros_like(acc)
+    first_t[...] = jnp.zeros_like(first_t)
+    for copy in copies:
+        copy.wait_send()
+    low_wait(0)
+
+    @pl.loop(0, tiles)
+    def _(visit):
+        number = base + visit
+        tile = lax.rem(number, tiles)
+        slot = lax.rem(number, held)
+
+        @pl.when(visit >= held)
+        def _():
+            load(number).wait()
+
+        add_first(tile, kept.at[tile])
+        add_second(0, tile, slot)
+
+        @pl.when(visit < base)
+        def _():
+            load(number + held).start()
+
+    copies = exchange(0)
+    finals = []
+    for d in range(1, n_out):
+        copy = pltpu.make_async_remote_copy(
+            src_ref=lamq, dst_ref=finrecv.at[d],
+            send_sem=fs.at[d], recv_sem=fr.at[d],
+            device_id=(lax.rem(o + d, n_out), c), device_id_type=MESH)
+        copy.start()
+        finals.append(copy)
+    out_ref[pl.ds(pl.multiple_of(o * quarter, quarter), quarter)] = lamq[...]
+    for d in range(1, n_out):
+        finals[d - 1].wait_recv()
+        source = lax.rem(o + n_out - d, n_out)
+        out_ref[pl.ds(pl.multiple_of(source * quarter, quarter), quarter)] = finrecv[d]
+    for copy in copies + finals:
+        copy.wait_send()
+
+
+def per_device(n_out, n_in, tensor, linear, adjoint_end, states):
+    rows, cols, modes = tensor.shape
+    steps, batch, _ = states.shape
+    fits = (steps == 2 and cols % 128 == 0 and rows % cols == 0 and batch % 128 == 0
+            and batch % (32 * n_out) == 0 and n_out > 1 and n_in > 1)
+    if not fits:
+        return plain(tensor, linear, adjoint_end, states)
+    ratio = rows // cols
+    tiles = rows // tile_modes
+    held = min(slots, tiles)
+    quarter = batch // n_out
+    dma = pltpu.SemaphoreType.DMA
+    vmem = pl.BlockSpec(memory_space=pltpu.VMEM)
+    return pl.pallas_call(
+        functools.partial(kernel, n_out, n_in, rows, cols),
+        out_shape=jax.ShapeDtypeStruct((batch, cols), jnp.float32),
+        in_specs=[pl.BlockSpec(memory_space=pl.ANY), vmem, vmem, vmem],
+        out_specs=vmem,
+        scratch_shapes=[
+            pltpu.VMEM((held, tile_modes * cols, modes), jnp.bfloat16),
+            pltpu.VMEM((tiles, tile_modes * cols, batch), jnp.float32),
+            pltpu.VMEM((modes, steps * batch), jnp.bfloat16),
+            pltpu.VMEM((steps, quarter, cols), jnp.bfloat16),
+            pltpu.VMEM((steps, ratio, n_out, quarter, cols), jnp.bfloat16),
+            pltpu.VMEM((ratio, batch, cols), jnp.float32),
+            pltpu.VMEM((rows, batch), jnp.float32),
+            pltpu.VMEM((batch, modes), jnp.float32),
+            pltpu.VMEM((cols, batch), jnp.float32),
+            pltpu.VMEM((n_in, batch, cols), jnp.bfloat16),
+            pltpu.VMEM((steps, n_in, batch, cols), jnp.bfloat16),
+            pltpu.VMEM((n_out, quarter, cols), jnp.float32),
+            pltpu.VMEM((steps, n_out, quarter, cols), jnp.float32),
+            pltpu.VMEM((quarter, cols), jnp.float32),
+            pltpu.VMEM((n_out, quarter, cols), jnp.float32),
+            dma((held,)),
+            dma((steps, n_in)), dma((steps, n_in)),
+            dma((steps, n_out)), dma((steps, n_out)),
+            dma((steps, n_in)), dma((steps, ratio, n_out)),
+            dma((n_out,)), dma((n_out,)),
+        ],
+        compiler_params=pltpu.CompilerParams(
+            collective_id=0, has_side_effects=True, vmem_limit_bytes=62 * 2**20),
+        cost_estimate=pl.CostEstimate(
+            flops=4 * steps * batch * rows * cols * modes,
+            bytes_accessed=2 * 2 * rows * cols * modes, transcendentals=0),
+    )(tensor.reshape(rows * cols, modes), linear, adjoint_end, states)
+
+
 def solution(mesh):
     placed = (P("out", "in", None), P("out", "in"), P(None, "in"), P())
     return jax.shard_map(
-        per_device, mesh=mesh, in_specs=placed, out_specs=P(None, "in"), check_vma=False
+        functools.partial(per_device, mesh.shape["out"], mesh.shape["in"]),
+        mesh=mesh, in_specs=placed, out_specs=P(None, "in"), check_vma=False
     )

time: 241 us -> 95 us (0.39)
  matrix products: 135 us -> 0 us
  Pallas kernels: 0 us -> 93.4 us
  waiting for transfers between devices: 67.5 us -> 0 us
  blocking collectives: 20.2 us -> 0 us
  between operations: 13.2 us -> 0.01 us
  other arithmetic: 3.25 us -> 0 us
    dot_general x8 -> x0, matrix products: 135 us -> none  [the longest x2 64.9 us: pieces(): lax.dot_general(state, flat, (((1,), (1,)), ((), ())), preferred_element_...]
    pallas_call x0 -> x1, Pallas kernels: none -> 93.4 us  [per_device(): pl.pallas_call(functools.partial(kernel, n_out, n_in, rows, cols), out_sh...]
    psum x2 -> x0, waiting for transfers between devices: 67.4 us -> none  [per_device(): total = lax.psum(local + second_own, 'out')]
    all_gather x2 -> x0, blocking collectives: 20.2 us -> none  [per_device(): lax.all_gather(lam_own.astype(jnp.bfloat16), 'in', axis=1, tiled=True)]
  transfers between devices with their start and end apart: 4 -> 0, of which waited for: 2 -> 0; matrix products, arithmetic and copies ran while one was open for 36% -> 0% of each run, Pallas kernels for 0% -> 0%
where the time goes in v1:
time: 95 us; the launch traced here: 94.9 us
  Pallas kernels  93.4 us (98%)
  local copies, waits for them, and re-layouts  1.47 us (2%)
    pallas_call x1, Pallas kernels, per_device(): pl.pallas_call(functools.partial(kernel, n_out, n_in, rows, cols), out_sh...  93.4 us

profile of v1, /device:TPU:0, one launch (start us, length us, event | category | flops | bytes accessed | tf_op | source)
XLA Modules:
  0.0 94.9 jit_solution(5791904466424713899)
XLA Ops:
  0.0 93.4 %shard_map.46 = f32[128,128]{1,0:T(8,128)} custom-call(bf16[32768,1024]{1,0:T(8,128)(2,1)} %bitcast.flat_ref, bf16[256,128]{1,0:T(8,128)(2,1)} %linear_ref.1, f32[128,128]{1,0:T(8,128)} %adjoint_ref.1, bf16[2,128,1024]{2,1,0:T(8,128)(2,1)} %states_ref.1), custom_call_target="tpu_custom_call" | custom-call | flops 34359738368 | bytes 134217728 | tf_op jit(solution)/shard_map/pallas_call | solution.py:262
  93.4 1.5 %copy.6 = f32[128,128]{1,0:T(8,128)} copy(f32[128,128]{1,0:T(8,128)} %shard_map.46) | data formatting | bytes 131072

commit v2 on v1

--- a/solution.py
+++ b/solution.py
@@ -9,8 +9,10 @@
 
 step_size = 0.5
 MESH = pl.DeviceIdType.MESH
-tile_modes = 8
-slots = 18
+tile_modes = 16
+slots = 10
+lead = 3
+trail = 4
 
 
 def pieces(tensor, linear, state, full_low):
@@ -49,7 +51,7 @@
 
 def kernel(n_out, n_in, rows, cols,
            flat_ref, linear_ref, adjoint_ref, states_ref, out_ref,
-           tbuf, kept, st, lowsrc, lowbuf, lowf, low_t, acc, first_t,
+           tbuf, kept, early, st, lowsrc, lowbuf, lowf, low_t, acc, first_t,
            send1, recv1, part2, recv2, lamq, finrecv,
            tsem, s1, r1, s2, r2, ls, lr, fs, fr):
     batch = adjoint_ref.shape[0]
@@ -59,6 +61,8 @@
     tile_rows = tile_modes * cols
     held = tbuf.shape[0]
     base = tiles - held
+    begin = early.shape[0]
+    end = max(tiles - trail, begin)
     o = lax.axis_index("out")
     c = lax.axis_index("in")
     plane = c // ratio
@@ -87,6 +91,11 @@
             @pl.when(jnp.logical_or(o != q, c != source))
             def _():
                 pl.semaphore_signal(barrier, inc=1, device_id=(q, source), device_id_type=MESH)
+
+    st[:, :batch] = states_ref[1].T
+    st[:, batch:] = states_ref[0].T
+    acc[...] = jnp.zeros_like(acc)
+    first_t[...] = jnp.zeros_like(first_t)
 
     @pl.when(plane == o)
     def _():
@@ -144,10 +153,20 @@
         low = low_t[pl.ds(pl.multiple_of(tile * tile_modes, tile_modes), tile_modes)]
         total = first_t[...]
         for q in range(tile_modes):
-            total += low[q:q + 1] * projected[q * cols:(q + 1) * cols]
+            total += low[q:q + 1] * projected[q * cols:(q + 1) * cols].astype(jnp.float32)
         first_t[...] = total
 
-    def exchange(step):
+    def project(tile, slot):
+        both = jnp.dot(tbuf[slot], st[...], preferred_element_type=jnp.float32)
+        kept[tile] = both[:, batch:].astype(jnp.bfloat16)
+        return both[:, :batch]
+
+    def refill(tile):
+        @pl.when(tile < base)
+        def _():
+            load(tile + held).start()
+
+    def exchange(step, between):
         for x in range(n_in):
             send1[x] = acc[:, x * cols:(x + 1) * cols].astype(jnp.bfloat16)
         copies = []
@@ -159,6 +178,7 @@
                 device_id=(o, target), device_id_type=MESH)
             copy.start()
             copies.append(copy)
+        between()
         total = first_t[...].T + acc[:, pl.ds(pl.multiple_of(c * cols, cols), cols)]
         for e in range(ratio):
             total += jnp.dot(lowbuf[step, e].reshape(batch, cols), linear_ref[e * cols:(e + 1) * cols],
@@ -184,26 +204,44 @@
 
     lamq[...] = adjoint_ref[pl.ds(pl.multiple_of(o * quarter, quarter), quarter)]
     low_start(1)
-    st[:, :batch] = states_ref[1].T
-    st[:, batch:] = states_ref[0].T
-    acc[...] = jnp.zeros_like(acc)
-    first_t[...] = jnp.zeros_like(first_t)
+
+    @pl.loop(0, begin)
+    def _(tile):
+        load(tile).wait()
+        early[tile] = project(tile, lax.rem(tile, held))
+
     low_wait(1)
 
-    @pl.loop(0, tiles)
+    @pl.loop(0, begin)
+    def _(tile):
+        add_first(tile, early.at[tile])
+        add_second(1, tile, lax.rem(tile, held))
+        refill(tile)
+
+    @pl.loop(begin, end)
     def _(tile):
         slot = lax.rem(tile, held)
         load(tile).wait()
-        both = jnp.dot(tbuf[slot], st[...], preferred_element_type=jnp.float32)
-        kept[tile] = both[:, batch:]
-        add_first(tile, both[:, :batch])
+        add_first(tile, project(tile, slot))
         add_second(1, tile, slot)
-
-        @pl.when(tile < base)
-        def _():
-            load(tile + held).start()
-
-    copies = exchange(1)
+        refill(tile)
+
+    @pl.loop(end, tiles)
+    def _(tile):
+        load(tile).wait()
+        add_second(1, tile, lax.rem(tile, held))
+
+    def rest_of_projection():
+        @pl.loop(end, tiles)
+        def _(tile):
+            add_first(tile, project(tile, lax.rem(tile, held)))
+
+    def kept_first():
+        @pl.loop(0, tiles)
+        def _(tile):
+            add_first(tile, kept.at[tile])
+
+    copies = exchange(1, rest_of_projection)
     low_start(0)
     acc[...] = jnp.zeros_like(acc)
     first_t[...] = jnp.zeros_like(first_t)
@@ -221,14 +259,13 @@
         def _():
             load(number).wait()
 
-        add_first(tile, kept.at[tile])
         add_second(0, tile, slot)
 
         @pl.when(visit < base)
         def _():
             load(number + held).start()
 
-    copies = exchange(0)
+    copies = exchange(0, kept_first)
     finals = []
     for d in range(1, n_out):
         copy = pltpu.make_async_remote_copy(
@@ -250,7 +287,8 @@
     rows, cols, modes = tensor.shape
     steps, batch, _ = states.shape
     fits = (steps == 2 and cols % 128 == 0 and rows % cols == 0 and batch % 128 == 0
-            and batch % (32 * n_out) == 0 and n_out > 1 and n_in > 1)
+            and batch % (32 * n_out) == 0 and n_out > 1 and n_in > 1
+            and rows % tile_modes == 0 and rows // tile_modes - trail >= slots - trail >= lead)
     if not fits:
         return plain(tensor, linear, adjoint_end, states)
     ratio = rows // cols
@@ -266,7 +304,8 @@
         out_specs=vmem,
         scratch_shapes=[
             pltpu.VMEM((held, tile_modes * cols, modes), jnp.bfloat16),
-            pltpu.VMEM((tiles, tile_modes * cols, batch), jnp.float32),
+            pltpu.VMEM((tiles, tile_modes * cols, batch), jnp.bfloat16),
+            pltpu.VMEM((min(lead, held), tile_modes * cols, batch), jnp.float32),
             pltpu.VMEM((modes, steps * batch), jnp.bfloat16),
             pltpu.VMEM((steps, quarter, cols), jnp.bfloat16),
             pltpu.VMEM((steps, ratio, n_out, quarter, cols), jnp.bfloat16),

time: 95 us -> 81 us (0.85)
  Pallas kernels: 93.4 us -> 79.4 us
    pallas_call x1, Pallas kernels: 93.4 us -> 79.4 us  [per_device(): pl.pallas_call(functools.partial(kernel, n_out, n_in, rows, cols), out_sh...]
where the time goes in v2:
time: 81 us; the launch traced here: 80.9 us
  Pallas kernels  79.4 us (98%)
  local copies, waits for them, and re-layouts  1.47 us (2%)
    pallas_call x1, Pallas kernels, per_device(): pl.pallas_call(functools.partial(kernel, n_out, n_in, rows, cols), out_sh...  79.4 us

profile of v2, /device:TPU:0, one launch (start us, length us, event | category | flops | bytes accessed | tf_op | source)
XLA Modules:
  0.0 80.9 jit_solution(14571046860833656839)
XLA Ops:
  0.0 79.4 %shard_map.46 = f32[128,128]{1,0:T(8,128)} custom-call(bf16[32768,1024]{1,0:T(8,128)(2,1)} %bitcast.flat_ref, bf16[256,128]{1,0:T(8,128)(2,1)} %linear_ref.1, f32[128,128]{1,0:T(8,128)} %adjoint_ref.1, bf16[2,128,1024]{2,1,0:T(8,128)(2,1)} %states_ref.1), custom_call_target="tpu_custom_call" | custom-call | flops 34359738368 | bytes 134217728 | tf_op jit(solution)/shard_map/pallas_call | solution.py:300
  79.4 1.5 %copy.6 = f32[128,128]{1,0:T(8,128)} copy(f32[128,128]{1,0:T(8,128)} %shard_map.46) | data formatting | bytes 131072

commit v3 on v2

--- a/solution.py
+++ b/solution.py
@@ -10,6 +10,8 @@
 step_size = 0.5
 MESH = pl.DeviceIdType.MESH
 tile_modes = 16
+group = 4
+out_width = 256
 slots = 10
 lead = 3
 trail = 4
@@ -147,7 +149,11 @@
         own = states_ref[step, :, pl.ds(pl.multiple_of(c * cols, cols), cols)].astype(jnp.float32)
         pair = jnp.concatenate(
             [(turned[:, q:q + 1] * own).astype(jnp.bfloat16) for q in range(tile_modes)], axis=1)
-        acc[...] += jnp.dot(pair, tbuf[slot], preferred_element_type=jnp.float32)
+        modes = acc.shape[1]
+        width = min(out_width, modes)
+        for x in range(0, modes, width):
+            acc[:, x:x + width] += jnp.dot(
+                pair, tbuf[slot, :, x:x + width], preferred_element_type=jnp.float32)
 
     def add_first(tile, projected):
         low = low_t[pl.ds(pl.multiple_of(tile * tile_modes, tile_modes), tile_modes)]
@@ -156,10 +162,21 @@
             total += low[q:q + 1] * projected[q * cols:(q + 1) * cols].astype(jnp.float32)
         first_t[...] = total
 
-    def project(tile, slot):
-        both = jnp.dot(tbuf[slot], st[...], preferred_element_type=jnp.float32)
-        kept[tile] = both[:, batch:].astype(jnp.bfloat16)
-        return both[:, :batch]
+    def project(tile, slot, store=None):
+        if store is None:
+            low = low_t[pl.ds(pl.multiple_of(tile * tile_modes, tile_modes), tile_modes)]
+            total = first_t[...]
+        for x in range(0, tile_modes, group):
+            span = slice(x * cols, (x + group) * cols)
+            both = jnp.dot(tbuf[slot, span], st[...], preferred_element_type=jnp.float32)
+            kept[tile, span] = both[:, batch:].astype(jnp.bfloat16)
+            if store is not None:
+                store[span] = both[:, :batch]
+            else:
+                for q in range(group):
+                    total += low[x + q:x + q + 1] * both[q * cols:(q + 1) * cols, :batch]
+        if store is None:
+            first_t[...] = total
 
     def refill(tile):
         @pl.when(tile < base)
@@ -208,7 +225,7 @@
     @pl.loop(0, begin)
     def _(tile):
         load(tile).wait()
-        early[tile] = project(tile, lax.rem(tile, held))
+        project(tile, lax.rem(tile, held), early.at[tile])
 
     low_wait(1)
 
@@ -222,7 +239,7 @@
     def _(tile):
         slot = lax.rem(tile, held)
         load(tile).wait()
-        add_first(tile, project(tile, slot))
+        project(tile, slot)
         add_second(1, tile, slot)
         refill(tile)
 
@@ -234,7 +251,7 @@
     def rest_of_projection():
         @pl.loop(end, tiles)
         def _(tile):
-            add_first(tile, project(tile, lax.rem(tile, held)))
+            project(tile, lax.rem(tile, held))
 
     def kept_first():
         @pl.loop(0, tiles)

time: 81 us -> 81 us (level)
  no operation moved by 1% of the time
where the time goes in v3:
time: 81 us; the launch traced here: 80.8 us
  Pallas kernels  79.3 us (98%)
  local copies, waits for them, and re-layouts  1.47 us (2%)
    pallas_call x1, Pallas kernels, per_device(): pl.pallas_call(functools.partial(kernel, n_out, n_in, rows, cols), out_sh...  79.3 us

profile of v3, /device:TPU:0, one launch (start us, length us, event | category | flops | bytes accessed | tf_op | source)
XLA Modules:
  0.0 80.8 jit_solution(10148729780996035451)
XLA Ops:
  0.0 79.3 %shard_map.46 = f32[128,128]{1,0:T(8,128)} custom-call(bf16[32768,1024]{1,0:T(8,128)(2,1)} %bitcast.flat_ref, bf16[256,128]{1,0:T(8,128)(2,1)} %linear_ref.1, f32[128,128]{1,0:T(8,128)} %adjoint_ref.1, bf16[2,128,1024]{2,1,0:T(8,128)(2,1)} %states_ref.1), custom_call_target="tpu_custom_call" | custom-call | flops 34359738368 | bytes 134217728 | tf_op jit(solution)/shard_map/pallas_call | solution.py:317
  79.4 1.5 %copy.6 = f32[128,128]{1,0:T(8,128)} copy(f32[128,128]{1,0:T(8,128)} %shard_map.46) | data formatting | bytes 131072

commit v4 on v3

--- a/solution.py
+++ b/solution.py
@@ -13,7 +13,7 @@
 group = 4
 out_width = 256
 slots = 10
-lead = 3
+lead = 4
 trail = 4
 
 
@@ -53,7 +53,7 @@
 
 def kernel(n_out, n_in, rows, cols,
            flat_ref, linear_ref, adjoint_ref, states_ref, out_ref,
-           tbuf, kept, early, st, lowsrc, lowbuf, lowf, low_t, acc, first_t,
+           tbuf, kept, early, pair_a, pair_b, st, lowsrc, lowbuf, lowf, low_t, acc, first_t,
            send1, recv1, part2, recv2, lamq, finrecv,
            tsem, s1, r1, s2, r2, ls, lr, fs, fr):
     batch = adjoint_ref.shape[0]
@@ -142,18 +142,46 @@
             def _():
                 low_copy(step, x).wait_send()
 
-    def add_second(step, tile, slot):
+    def pair_of(step, tile):
         per = cols // tile_modes
         offset = lax.rem(tile, per) * tile_modes
         turned = pltpu.roll(lowf[tile // per], lax.rem(cols - offset, cols), 1)
         own = states_ref[step, :, pl.ds(pl.multiple_of(c * cols, cols), cols)].astype(jnp.float32)
-        pair = jnp.concatenate(
-            [(turned[:, q:q + 1] * own).astype(jnp.bfloat16) for q in range(tile_modes)], axis=1)
+        return [(turned[:, q:q + 1] * own).astype(jnp.bfloat16) for q in range(tile_modes)]
+
+    def make_pair(step, tile, ref):
+        for q, block in enumerate(pair_of(step, tile)):
+            ref[:, q * cols:(q + 1) * cols] = block
+
+    def use_pair(ref, slot):
+        modes = acc.shape[1]
+        width = min(out_width, modes)
+        for x in range(0, modes, width):
+            acc[:, x:x + width] += jnp.dot(
+                ref[...], tbuf[slot, :, x:x + width], preferred_element_type=jnp.float32)
+
+    def add_second(step, tile, slot):
+        pair = jnp.concatenate(pair_of(step, tile), axis=1)
         modes = acc.shape[1]
         width = min(out_width, modes)
         for x in range(0, modes, width):
             acc[:, x:x + width] += jnp.dot(
                 pair, tbuf[slot, :, x:x + width], preferred_element_type=jnp.float32)
+
+    def second_run(step, start, stop, before, after):
+        make_pair(step, lax.rem(start, tiles), pair_a)
+
+        @pl.loop(0, (stop - start) // 2)
+        def _(turn):
+            number = start + 2 * turn
+            before(number)
+            before(number + 1)
+            make_pair(step, lax.rem(number + 1, tiles), pair_b)
+            use_pair(pair_a, lax.rem(number, held))
+            make_pair(step, lax.rem(number + 2, tiles), pair_a)
+            use_pair(pair_b, lax.rem(number + 1, held))
+            after(number)
+            after(number + 1)
 
     def add_first(tile, projected):
         low = low_t[pl.ds(pl.multiple_of(tile * tile_modes, tile_modes), tile_modes)]
@@ -229,11 +257,11 @@
 
     low_wait(1)
 
-    @pl.loop(0, begin)
-    def _(tile):
+    def after_early(tile):
         add_first(tile, early.at[tile])
-        add_second(1, tile, lax.rem(tile, held))
         refill(tile)
+
+    second_run(1, 0, begin, lambda tile: None, after_early)
 
     @pl.loop(begin, end)
     def _(tile):
@@ -243,10 +271,7 @@
         add_second(1, tile, slot)
         refill(tile)
 
-    @pl.loop(end, tiles)
-    def _(tile):
-        load(tile).wait()
-        add_second(1, tile, lax.rem(tile, held))
+    second_run(1, end, tiles, lambda tile: load(tile).wait(), lambda tile: None)
 
     def rest_of_projection():
         @pl.loop(end, tiles)
@@ -266,21 +291,17 @@
         copy.wait_send()
     low_wait(0)
 
-    @pl.loop(0, tiles)
-    def _(visit):
-        number = base + visit
-        tile = lax.rem(number, tiles)
-        slot = lax.rem(number, held)
-
-        @pl.when(visit >= held)
+    def wait_again(number):
+        @pl.when(number >= tiles)
         def _():
             load(number).wait()
 
-        add_second(0, tile, slot)
-
-        @pl.when(visit < base)
+    def load_again(number):
+        @pl.when(number < 2 * base)
         def _():
             load(number + held).start()
+
+    second_run(0, base, base + tiles, wait_again, load_again)
 
     copies = exchange(0, kept_first)
     finals = []
@@ -305,7 +326,8 @@
     steps, batch, _ = states.shape
     fits = (steps == 2 and cols % 128 == 0 and rows % cols == 0 and batch % 128 == 0
             and batch % (32 * n_out) == 0 and n_out > 1 and n_in > 1
-            and rows % tile_modes == 0 and rows // tile_modes - trail >= slots - trail >= lead)
+            and rows % tile_modes == 0 and rows // tile_modes >= slots >= lead + trail
+            and rows // tile_modes % 2 == 0)
     if not fits:
         return plain(tensor, linear, adjoint_end, states)
     ratio = rows // cols
@@ -323,6 +345,8 @@
             pltpu.VMEM((held, tile_modes * cols, modes), jnp.bfloat16),
             pltpu.VMEM((tiles, tile_modes * cols, batch), jnp.bfloat16),
             pltpu.VMEM((min(lead, held), tile_modes * cols, batch), jnp.float32),
+            pltpu.VMEM((batch, tile_modes * cols), jnp.bfloat16),
+            pltpu.VMEM((batch, tile_modes * cols), jnp.bfloat16),
             pltpu.VMEM((modes, steps * batch), jnp.bfloat16),
             pltpu.VMEM((steps, quarter, cols), jnp.bfloat16),
             pltpu.VMEM((steps, ratio, n_out, quarter, cols), jnp.bfloat16),

time: 81 us -> 74.2 us (0.916)
  Pallas kernels: 79.3 us -> 72.6 us
    pallas_call x1, Pallas kernels: 79.3 us -> 72.6 us  [per_device(): pl.pallas_call(functools.partial(kernel, n_out, n_in, rows, cols), out_sh...]
where the time goes in v4:
time: 74.2 us; the launch traced here: 74.1 us
  Pallas kernels  72.6 us (98%)
  local copies, waits for them, and re-layouts  1.47 us (2%)
    pallas_call x1, Pallas kernels, per_device(): pl.pallas_call(functools.partial(kernel, n_out, n_in, rows, cols), out_sh...  72.6 us

profile of v4, /device:TPU:0, one launch (start us, length us, event | category | flops | bytes accessed | tf_op | source)
XLA Modules:
  0.0 74.1 jit_solution(10814464266305583264)
XLA Ops:
  0.0 72.6 %shard_map.46 = f32[128,128]{1,0:T(8,128)} custom-call(bf16[32768,1024]{1,0:T(8,128)(2,1)} %bitcast.flat_ref, bf16[256,128]{1,0:T(8,128)(2,1)} %linear_ref.1, f32[128,128]{1,0:T(8,128)} %adjoint_ref.1, bf16[2,128,1024]{2,1,0:T(8,128)(2,1)} %states_ref.1), custom_call_target="tpu_custom_call" | custom-call | flops 34359738368 | bytes 134217728 | tf_op jit(solution)/shard_map/pallas_call | solution.py:339
  72.6 1.5 %copy.6 = f32[128,128]{1,0:T(8,128)} copy(f32[128,128]{1,0:T(8,128)} %shard_map.46) | data formatting | bytes 131072
